TPU v7x, 256 devices: a whole 4x4x8 slice. The times are simulated.
256 devices in a mesh: tm: 32 (over z_lo, x, core), tp: 8 (over y, z_hi).
Axes of the slice: x: 4, y: 4, z: 8 (z_hi: 2, z_lo: 4; z = z_hi * 4 + z_lo), core: 2. Of those that a mesh axis runs over, the one named last changes fastest.
Arguments:
- trajectory: float32 [64, 128, 64], P('tm', 'tp'), may hold values from -6 to 6
- window_start: int32 [1], replicated, may hold values from 0 to 48
- step_sizes: float32 [112], replicated, may hold values from 0.02 to 0.1
- modulation: bfloat16 [112, 10, 1536], replicated, may hold values from -4 to 4
- context: bfloat16 [128, 1536], replicated, may hold values from -6 to 6
- position_embed: bfloat16 [128, 1536], P('tp'), may hold values from -2 to 2
- patch_weight: bfloat16 [64, 1536], replicated, may hold values from -0.75 to 0.75
- heads_weight: bfloat16 [1536, 3, 1536], P(None, None, 'tp'), may hold values from -0.15625 to 0.15625
- query_gain: float32 [64], replicated, may hold values from 0.1 to 1.9
- key_gain: float32 [64], replicated, may hold values from 0.1 to 1.9
- text_weight: bfloat16 [1536, 2, 1536], P(None, None, 'tp'), may hold values from -0.15625 to 0.15625
- output_weight: bfloat16 [1536, 1536], P('tp'), may hold values from -0.15625 to 0.15625
- up_weight: bfloat16 [1536, 6144], P(None, 'tp'), may hold values from -0.15625 to 0.15625
- down_weight: bfloat16 [6144, 1536], P('tp'), may hold values from -0.078125 to 0.078125
- final_weight: bfloat16 [1536, 64], replicated, may hold values from -0.15625 to 0.15625
Outputs:
- trajectory_next: float32 [64, 128, 64], P('tm', 'tp')
All inputs are finite; a program needn't handle non-finite values.
Results may differ from a plain program's by a relative error of at most 0.0085.
Values may be sent and summed in bfloat16 or wider, within the bound.
A program may use at most 64 MiB of HBM per device.

v0:
```python
import jax
import jax.numpy as jnp
from jax import lax
from jax.sharding import PartitionSpec as P

ITERS = 3


EPSILON = 1e-06


def spread_2(value, axis, root):
    mine = lax.axis_index(axis) == root
    return lax.psum(jnp.where(mine, value, jnp.zeros_like(value)), axis)


def carried_in(value, axis, join, neutral):
    count, mine = (lax.axis_size(axis), lax.axis_index(axis))
    pieces = lax.all_gather(value, axis)
    so_far = jnp.full_like(value, 0) + jnp.asarray(neutral, value.dtype)

    def step(position, so_far):
        longer = join(so_far, pieces[position])
        return jnp.where(position < mine, longer, so_far)

    return lax.fori_loop(0, count - 1, step, so_far)


def layer_norm(values):
    average = jnp.mean(values, axis=-1, keepdims=True)
    centered = values - average
    spread = jnp.mean(centered * centered, axis=-1, keepdims=True)
    return centered * lax.rsqrt(spread + EPSILON)


def modulate(values, shift_by, scale_by):
    return (layer_norm(values) * (1.0 + scale_by) + shift_by).astype(jnp.bfloat16)


def head_norm(values, gain_vector):
    square = jnp.mean(values * values, axis=-1, keepdims=True)
    return (values * lax.rsqrt(square + EPSILON) * gain_vector).astype(jnp.bfloat16)


def add_terms(earlier, later):
    return earlier + later


def per_device(
    trajectory,
    window_start,
    step_sizes,
    modulation,
    context,
    position_embed,
    patch_weight,
    heads_weight,
    query_gain,
    key_gain,
    text_weight,
    output_weight,
    up_weight,
    down_weight,
    final_weight,
):
    time_slots = trajectory.shape[0]
    row_share = trajectory.shape[1]
    patch_size = trajectory.shape[2]
    model_width = patch_weight.shape[1]
    local_width = output_weight.shape[0]
    head_dim = query_gain.shape[0]
    local_heads = local_width // head_dim
    seq_total = row_share * lax.axis_size("tp")
    text_count = context.shape[0]
    score_scale = head_dim ** (-0.5)
    time_index = lax.axis_index("tm")
    first_entry = window_start[0] + time_index * time_slots
    slot_steps = lax.dynamic_slice_in_dim(step_sizes, first_entry, time_slots)
    slot_table = lax.dynamic_slice_in_dim(modulation, first_entry, time_slots).astype(jnp.float32)[
        None
    ]
    heads_flat = heads_weight.reshape(model_width, 3 * local_width)
    text_normed = modulate(
        context.astype(jnp.float32)[:, None, :], slot_table[:, :, 6], slot_table[:, :, 7]
    )
    text_joint = jnp.dot(
        text_normed.reshape(-1, model_width),
        text_weight.reshape(model_width, 2 * local_width),
        preferred_element_type=jnp.float32,
    )
    text_joint = text_joint.reshape(text_count, time_slots, 2 * local_width)
    text_keys = head_norm(
        text_joint[..., :local_width].reshape(text_count, time_slots, local_heads, head_dim),
        key_gain,
    )
    text_values = (
        text_joint[..., local_width:]
        .astype(jnp.bfloat16)
        .reshape(text_count, time_slots, local_heads, head_dim)
    )
    position = position_embed.astype(jnp.float32)[:, None, :]
    own_first = trajectory[0]
    anchor = spread_2(own_first, "tm", 0)
    states = jnp.transpose(trajectory, (1, 0, 2))
    outcome = trajectory
    for repeat in range(ITERS):
        hidden = jnp.dot(
            states.astype(jnp.bfloat16).reshape(-1, patch_size),
            patch_weight,
            preferred_element_type=jnp.float32,
        )
        hidden = hidden.reshape(row_share, time_slots, model_width) + position
        normed = modulate(hidden, slot_table[:, :, 0], slot_table[:, :, 1])
        row_piece = lax.all_gather(normed, "tp", axis=0, tiled=True)
        product = jnp.dot(
            row_piece.reshape(-1, model_width), heads_flat, preferred_element_type=jnp.float32
        )
        joint = product.reshape(row_piece.shape[0], time_slots, 3 * local_width)
        query = head_norm(
            joint[..., :local_width].reshape(seq_total, time_slots, local_heads, head_dim),
            query_gain,
        )
        image_keys = head_norm(
            joint[..., local_width : 2 * local_width].reshape(
                seq_total, time_slots, local_heads, head_dim
            ),
            key_gain,
        )
        image_values = (
            joint[..., 2 * local_width :]
            .astype(jnp.bfloat16)
            .reshape(seq_total, time_slots, local_heads, head_dim)
        )
        all_keys = jnp.concatenate([image_keys, text_keys], axis=0)
        all_values = jnp.concatenate([image_values, text_values], axis=0)
        scores = (
            jnp.einsum("qshd,kshd->shqk", query, all_keys, preferred_element_type=jnp.float32)
            * score_scale
        )
        powers = jnp.exp(scores)
        probs = (powers / jnp.sum(powers, axis=-1, keepdims=True)).astype(jnp.bfloat16)
        attended = jnp.einsum(
            "shqk,kshd->qshd", probs, all_values, preferred_element_type=jnp.float32
        )
        attended = attended.astype(jnp.bfloat16).reshape(seq_total, time_slots, local_width)
        project_product = jnp.dot(
            attended.reshape(-1, local_width), output_weight, preferred_element_type=jnp.float32
        )
        mixed = lax.psum_scatter(
            project_product.reshape(
                row_share * lax.axis_size("tp"), time_slots, model_width
            ).astype(jnp.bfloat16),
            "tp",
            scatter_dimension=0,
            tiled=True,
        ).astype(jnp.float32)
        hidden = hidden + slot_table[:, :, 2] * mixed
        normed = modulate(hidden, slot_table[:, :, 3], slot_table[:, :, 4])
        expand_row_piece = lax.all_gather(normed, "tp", axis=0, tiled=True)
        expand_product = jnp.dot(
            expand_row_piece.reshape(-1, model_width), up_weight, preferred_element_type=jnp.float32
        )
        activated_rows = jax.nn.gelu(expand_product, approximate=True).astype(jnp.bfloat16)
        activated = activated_rows.reshape(
            expand_row_piece.shape[0], time_slots, up_weight.shape[1]
        )
        contract_product = jnp.dot(
            activated.reshape(-1, activated.shape[2]),
            down_weight,
            preferred_element_type=jnp.float32,
        )
        hidden = hidden + slot_table[:, :, 5] * lax.psum_scatter(
            contract_product.reshape(
                row_share * lax.axis_size("tp"), time_slots, model_width
            ).astype(jnp.bfloat16),
            "tp",
            scatter_dimension=0,
            tiled=True,
        ).astype(jnp.float32)
        final_normed = modulate(hidden, slot_table[:, :, 8], slot_table[:, :, 9])
        drift = jnp.dot(
            final_normed.reshape(-1, model_width), final_weight, preferred_element_type=jnp.float32
        )
        terms = drift.reshape(row_share, time_slots, patch_size) * slot_steps[None, :, None]
        running = jnp.zeros((row_share, patch_size), jnp.float32)
        earlier_sums = []
        for offset in range(time_slots):
            earlier_sums.append(running)
            running = running + terms[:, offset]
        base = anchor - carried_in(running, "tm", add_terms, jnp.zeros_like(running))
        if repeat + 1 < ITERS:
            states = jnp.stack(
                [base - earlier_sums[offset] for offset in range(time_slots)], axis=1
            )
        else:
            outcome = jnp.stack(
                [base - (earlier_sums[offset] + terms[:, offset]) for offset in range(time_slots)],
                axis=0,
            )
    return outcome


def solution(mesh):
    return jax.shard_map(
        per_device,
        mesh=mesh,
        in_specs=(
            P("tm", "tp", None),
            P(),
            P(),
            P(),
            P(),
            P("tp", None),
            P(),
            P(None, None, "tp"),
            P(),
            P(),
            P(None, None, "tp"),
            P("tp", None),
            P(None, "tp"),
            P("tp", None),
            P(),
        ),
        out_specs=P("tm", "tp", None),
        check_vma=False,
    )
```

profile of v0, /device:TPU:1, one launch (start us, length us, event | category | flops | bytes accessed | tf_op | source)
XLA Modules:
  0.0 1086.3 jit_solution(9553754403534977093)
XLA Ops:
  11.6 54.7 %all_gather.30 = bf16[128,2,1536]{2,0,1:T(8,128)(2,1)S(1)} all-gather(bf16[16,2,1536]{2,0,1:T(8,128)(2,1)S(1)} %add_convert_fusion.10), channel_id=1, replica_groups=mesh['tm'=32,'tp'=8] {'tp'}, dimensions={0}, use_global_device_ids=true | all-gather | bytes 884736 | tf_op jit(solution)/shard_map/all_gather | solution.py:114
  72.9 2.2 fusion.2
  78.3 89.0 %reduce-scatter.7.cloned.1.call-done = bf16[16,2,1536]{2,0,1:T(8,128)(2,1)} async-done(((bf16[128,2,1536]{2,0,1:T(8,128)(2,1)}), bf16[16,2,1536]{2,0,1:T(8,128)(2,1)}) %reduce-scatter.7.cloned.1.call-update) | async-done | bytes 98320 | tf_op jit(solution)/shard_map/reduce_scatter | solution.py:149
  168.6 45.3 %all_gather.31 = bf16[128,2,1536]{2,0,1:T(8,128)(2,1)S(1)} all-gather(bf16[16,2,1536]{2,0,1:T(8,128)(2,1)S(1)} %add_convert_fusion.9), channel_id=1, replica_groups=mesh['tm'=32,'tp'=8] {'tp'}, dimensions={0}, use_global_device_ids=true | all-gather | bytes 884736 | tf_op jit(solution)/shard_map/all_gather | solution.py:159
  215.6 3.0 reshape.408
  218.6 4.6 convolution_convert_fusion.2
  223.2 2.9 convert_element_type.174
  226.1 2.1 copy.25
  228.4 79.2 %psum.7 = f32[16,64]{1,0:T(8,128)S(1)} all-reduce(f32[16,64]{1,0:T(8,128)S(1)} %select_bitcast_fusion), channel_id=1, replica_groups=mesh['tm'=32,'tp'=8] {'tm'}, use_global_device_ids=true, to_apply=%region_0.0 | all-reduce | flops 1024 | bytes 8192 | tf_op jit(solution)/shard_map/psum | solution.py:14
  307.6 9.9 reduce-scatter.9.cloned.1.call-done
  320.8 43.8 %all-gather = f32[512,1,64]{2,0,1:T(8,128)S(1)} all-gather(f32[16,1,64]{2,0,1:T(8,128)S(1)} %slice_add_fusion.5), channel_id=2, replica_groups=mesh['tm'=32,'tp'=8] {'tm'}, dimensions={0}, use_global_device_ids=true | all-gather | bytes 135168 | tf_op jit(solution)/shard_map/all_gather | solution.py:19
  368.0 46.0 %all_gather.33 = bf16[128,2,1536]{2,0,1:T(8,128)(2,1)S(1)} all-gather(bf16[16,2,1536]{2,0,1:T(8,128)(2,1)S(1)} %add_convert_fusion.7), channel_id=1, replica_groups=mesh['tm'=32,'tp'=8] {'tp'}, dimensions={0}, use_global_device_ids=true | all-gather | bytes 884736 | tf_op jit(solution)/shard_map/all_gather | solution.py:114
  414.0 2.2 fusion.146
  421.5 80.4 %reduce-scatter.11.cloned.1.call-done = bf16[16,2,1536]{2,0,1:T(8,128)(2,1)} async-done(((bf16[128,2,1536]{2,0,1:T(8,128)(2,1)}), bf16[16,2,1536]{2,0,1:T(8,128)(2,1)}) %reduce-scatter.11.cloned.1.call-update) | async-done | bytes 98320 | tf_op jit(solution)/shard_map/reduce_scatter | solution.py:149
  503.9 45.3 %all_gather.34 = bf16[128,2,1536]{2,0,1:T(8,128)(2,1)S(1)} all-gather(bf16[16,2,1536]{2,0,1:T(8,128)(2,1)S(1)} %add_convert_fusion.6), channel_id=1, replica_groups=mesh['tm'=32,'tp'=8] {'tp'}, dimensions={0}, use_global_device_ids=true | all-gather | bytes 884736 | tf_op jit(solution)/shard_map/all_gather | solution.py:159
  550.9 3.0 reshape.412
  553.8 4.6 convolution_convert_fusion.1
  558.4 2.9 convert_element_type.188
  561.3 2.1 copy.27
  563.5 89.2 %reduce-scatter.13.cloned.1.call-done = bf16[16,2,1536]{2,0,1:T(8,128)(2,1)} async-done(((bf16[128,2,1536]{2,0,1:T(8,128)(2,1)}), bf16[16,2,1536]{2,0,1:T(8,128)(2,1)}) %reduce-scatter.13.cloned.1.call-update) | async-done | bytes 98320 | tf_op jit(solution)/shard_map/reduce_scatter | solution.py:172
  656.6 46.4 %all-gather.1 = f32[512,1,64]{2,0,1:T(8,128)} all-gather(f32[16,1,64]{2,0,1:T(8,128)S(1)} %slice_add_fusion.4), channel_id=3, replica_groups=mesh['tm'=32,'tp'=8] {'tm'}, dimensions={0}, use_global_device_ids=true | all-gather | bytes 135168 | tf_op jit(solution)/shard_map/all_gather | solution.py:19
  703.0 40.7 %while.43 = (s32[]{:T(128)}, f32[16,64]{1,0:T(8,128)}, s32[]{:T(128)}, f32[32,16,64]{2,1,0:T(8,128)}, s32[]{:T(128)}, /*index=5*/s32[]{:T(128)}) while((s32[]{:T(128)}, f32[16,64]{1,0:T(8,128)}, s32[]{:T(128)}, f32[32,16,64]{2,1,0:T(8,128)}, s32[]{:T(128)}, /*index=5*/s32[]{:T(128)}) %tuple.132), condition=%wide.region_29.30_spmd.clone, body=%wide.region_28.29_spmd.clone.sunk | while | flops 3076 | bytes 12389 | solution.py:26
  746.6 45.9 %all_gather.36 = bf16[128,2,1536]{2,0,1:T(8,128)(2,1)S(1)} all-gather(bf16[16,2,1536]{2,0,1:T(8,128)(2,1)S(1)} %add_convert_fusion.4), channel_id=1, replica_groups=mesh['tm'=32,'tp'=8] {'tp'}, dimensions={0}, use_global_device_ids=true | all-gather | bytes 884736 | tf_op jit(solution)/shard_map/all_gather | solution.py:114
  792.5 2.2 fusion.147
  800.0 80.7 %reduce-scatter.15.cloned.1.call-done = bf16[16,2,1536]{2,0,1:T(8,128)(2,1)} async-done(((bf16[128,2,1536]{2,0,1:T(8,128)(2,1)}), bf16[16,2,1536]{2,0,1:T(8,128)(2,1)}) %reduce-scatter.15.cloned.1.call-update) | async-done | bytes 98320 | tf_op jit(solution)/shard_map/reduce_scatter | solution.py:149
  882.0 47.0 %all_gather.37 = bf16[128,2,1536]{2,0,1:T(8,128)(2,1)S(1)} all-gather(bf16[16,2,1536]{2,0,1:T(8,128)(2,1)S(1)} %add_convert_fusion.3), channel_id=1, replica_groups=mesh['tm'=32,'tp'=8] {'tp'}, dimensions={0}, use_global_device_ids=true | all-gather | bytes 884736 | tf_op jit(solution)/shard_map/all_gather | solution.py:159
  930.7 3.0 reshape.416
  933.7 4.6 convolution_convert_fusion
  938.2 2.9 convert_element_type.202
  941.1 2.1 copy.29
  943.3 87.4 %reduce-scatter.17.cloned.1.call-done = bf16[16,2,1536]{2,0,1:T(8,128)(2,1)} async-done(((bf16[128,2,1536]{2,0,1:T(8,128)(2,1)}), bf16[16,2,1536]{2,0,1:T(8,128)(2,1)}) %reduce-scatter.17.cloned.1.call-update) | async-done | bytes 98320 | tf_op jit(solution)/shard_map/reduce_scatter | solution.py:172
  1033.9 43.8 %all-gather.2 = f32[512,1,64]{2,0,1:T(8,128)S(1)} all-gather(f32[16,1,64]{2,0,1:T(8,128)S(1)} %slice_add_fusion.6), channel_id=4, replica_groups=mesh['tm'=32,'tp'=8] {'tm'}, dimensions={0}, use_global_device_ids=true | all-gather | bytes 135168 | tf_op jit(solution)/shard_map/all_gather | solution.py:19
  (281 shorter events, 93.9 us)
Async XLA Ops:
  6.5 212.1 %copy-start = (bf16[768,1536]{1,0:T(8,128)(2,1)S(1)}, bf16[768,1536]{1,0:T(8,128)(2,1)}, u32[]{:S(2)}) copy-start(bf16[768,1536]{1,0:T(8,128)(2,1)} %param.34) | copy-start | bytes 7077892
  6.5 160.8 %reduce-scatter.7.cloned.1.call-start = ((), (), s32[]{:S(2)}) async-start(), calls=%async_computation.6 | async-start | bytes 884736 | tf_op jit(solution)/shard_map/reduce_scatter | solution.py:149
  8.2 58.8 %copy-start.10 = (f32[16,1536]{1,0:T(8,128)}, f32[16,1536]{1,0:T(8,128)S(1)}, u32[]{:S(2)}) copy-start(f32[16,1536]{1,0:T(8,128)S(1)} %convert_element_type.159) | copy-start | bytes 294916
  8.2 58.2 %copy-start.1 = (bf16[1536,3,192]{0,2,1:T(8,128)(2,1)S(1)}, bf16[1536,3,192]{0,2,1:T(8,128)(2,1)}, u32[]{:S(2)}) copy-start(bf16[1536,3,192]{0,2,1:T(8,128)(2,1)} %param.28) | copy-start | bytes 5308420
  10.1 56.9 %copy-start.15 = (f32[2,1536]{1,0:T(2,128)}, f32[2,1536]{1,0:T(2,128)S(1)}, u32[]{:S(2)}) copy-start(f32[2,1536]{1,0:T(2,128)S(1)} %get-tuple-element.333) | copy-start | bytes 36868
  10.1 57.0 %copy-start.16 = (f32[2,1536]{1,0:T(2,128)}, f32[2,1536]{1,0:T(2,128)S(1)}, u32[]{:S(2)}) copy-start(f32[2,1536]{1,0:T(2,128)S(1)} %get-tuple-element.334) | copy-start | bytes 36868
  11.6 56.1 %copy-start.3 = (bf16[128,1536]{1,0:T(8,128)(2,1)S(1)}, bf16[128,1536]{1,0:T(8,128)(2,1)}, u32[]{:S(2)}) copy-start(bf16[128,1536]{1,0:T(8,128)(2,1)} %param.25) | copy-start | bytes 1179652
  71.4 5.5 copy-start.2
  75.1 92.2 %copy-start.21 = (f32[2,1536]{1,0:T(2,128)S(1)}, f32[2,1536]{1,0:T(2,128)}, u32[]{:S(2)}) copy-start(f32[2,1536]{1,0:T(2,128)} %get-tuple-element.335) | copy-start | bytes 36868
  75.1 93.4 %copy-start.11 = (f32[2,1536]{1,0:T(2,128)S(1)}, f32[2,1536]{1,0:T(2,128)}, u32[]{:S(2)}) copy-start(f32[2,1536]{1,0:T(2,128)} %get-tuple-element.329) | copy-start | bytes 36868
  75.1 93.4 %copy-start.13 = (f32[2,1536]{1,0:T(2,128)S(1)}, f32[2,1536]{1,0:T(2,128)}, u32[]{:S(2)}) copy-start(f32[2,1536]{1,0:T(2,128)} %get-tuple-element.330) | copy-start | bytes 36868
  78.2 239.3 %reduce-scatter.9.cloned.1.call-start = ((), (), s32[]{:S(2)}) async-start(), calls=%async_computation.7 | async-start | bytes 884736 | tf_op jit(solution)/shard_map/reduce_scatter | solution.py:172
  223.2 5.1 copy-start.34
  223.2 5.2 copy-start.27
  223.2 96.4 %copy-start.4 = (bf16[1536,64]{0,1:T(8,128)(2,1)S(1)}, bf16[1536,64]{0,1:T(8,128)(2,1)}, u32[]{:S(2)}) copy-start(bf16[1536,64]{0,1:T(8,128)(2,1)} %param.35) | copy-start | bytes 589828
  223.2 96.4 %copy-start.17 = (f32[2,1536]{1,0:T(2,128)S(1)}, f32[2,1536]{1,0:T(2,128)}, u32[]{:S(2)}) copy-start(f32[2,1536]{1,0:T(2,128)} %get-tuple-element.327) | copy-start | bytes 36868
  223.2 96.4 %copy-start.19 = (f32[2,1536]{1,0:T(2,128)S(1)}, f32[2,1536]{1,0:T(2,128)}, u32[]{:S(2)}) copy-start(f32[2,1536]{1,0:T(2,128)} %get-tuple-element.328) | copy-start | bytes 36868
  228.2 273.6 %reduce-scatter.11.cloned.1.call-start = ((), (), s32[]{:S(2)}) async-start(), calls=%async_computation.8 | async-start | bytes 884736 | tf_op jit(solution)/shard_map/reduce_scatter | solution.py:149
  228.4 92.3 %copy-start.29 = (f32[2]{0:T(128)}, f32[2]{0:T(128)S(1)}, u32[]{:S(2)}) copy-start(f32[2]{0:T(128)S(1)} %dynamic_slice.28) | copy-start | bytes 28
  307.6 58.2 %copy-start.23 = (f32[16,64]{1,0:T(8,128)}, f32[16,64]{1,0:T(8,128)S(1)}, u32[]{:S(2)}) copy-start(f32[16,64]{1,0:T(8,128)S(1)} %psum.7) | copy-start | bytes 12292
  414.0 4.3 copy-start.26
  421.4 231.3 %reduce-scatter.13.cloned.1.call-start = ((), (), s32[]{:S(2)}) async-start(), calls=%async_computation.9 | async-start | bytes 884736 | tf_op jit(solution)/shard_map/reduce_scatter | solution.py:172
  561.3 183.2 %copy-start.5 = (bf16[64,1536]{1,0:T(8,128)(2,1)S(1)}, bf16[64,1536]{1,0:T(8,128)(2,1)}, u32[]{:S(2)}) copy-start(bf16[64,1536]{1,0:T(8,128)(2,1)} %param.27) | copy-start | bytes 589828
  563.4 317.3 %reduce-scatter.15.cloned.1.call-start = ((), (), s32[]{:S(2)}) async-start(), calls=%async_computation.10 | async-start | bytes 884736 | tf_op jit(solution)/shard_map/reduce_scatter | solution.py:149
  796.8 83.9 %copy-start.22 = (f32[2,1536]{1,0:T(2,128)S(1)}, f32[2,1536]{1,0:T(2,128)}, u32[]{:S(2)}) copy-start(f32[2,1536]{1,0:T(2,128)} %get-tuple-element.335) | copy-start | bytes 36868
  796.8 85.1 %copy-start.12 = (f32[2,1536]{1,0:T(2,128)S(1)}, f32[2,1536]{1,0:T(2,128)}, u32[]{:S(2)}) copy-start(f32[2,1536]{1,0:T(2,128)} %get-tuple-element.329) | copy-start | bytes 36868
  796.8 85.1 %copy-start.14 = (f32[2,1536]{1,0:T(2,128)S(1)}, f32[2,1536]{1,0:T(2,128)}, u32[]{:S(2)}) copy-start(f32[2,1536]{1,0:T(2,128)} %get-tuple-element.330) | copy-start | bytes 36868
  800.0 230.7 %reduce-scatter.17.cloned.1.call-start = ((), (), s32[]{:S(2)}) async-start(), calls=%async_computation.11 | async-start | bytes 884736 | tf_op jit(solution)/shard_map/reduce_scatter | solution.py:172
  938.2 94.5 %copy-start.18 = (f32[2,1536]{1,0:T(2,128)S(1)}, f32[2,1536]{1,0:T(2,128)}, u32[]{:S(2)}) copy-start(f32[2,1536]{1,0:T(2,128)} %get-tuple-element.327) | copy-start | bytes 36868
  938.2 94.5 %copy-start.20 = (f32[2,1536]{1,0:T(2,128)S(1)}, f32[2,1536]{1,0:T(2,128)}, u32[]{:S(2)}) copy-start(f32[2,1536]{1,0:T(2,128)} %get-tuple-element.328) | copy-start | bytes 36868
  938.2 94.5 %copy-start.30 = (f32[2]{0:T(128)S(1)}, f32[2]{0:T(128)}, u32[]{:S(2)}) copy-start(f32[2]{0:T(128)} %copy-done.29) | copy-start | bytes 28
  941.1 137.7 %copy-start.24 = (f32[16,64]{1,0:T(8,128)S(1)}, f32[16,64]{1,0:T(8,128)}, u32[]{:S(2)}) copy-start(f32[16,64]{1,0:T(8,128)} %copy-done.23) | copy-start | bytes 12292
  (9 other events, 20.4 us)
Sparse Core Ops, SparseCore 0:
  78.4 88.8 reduce-scatter.6
  228.4 89.0 reduce-scatter.8
  421.5 80.2 reduce-scatter.10
  563.6 89.1 reduce-scatter.12
  800.1 80.5 reduce-scatter.14
  943.4 87.2 reduce-scatter.16
where the time goes:
time: 1090 us
  blocking collectives  497 us (46%)
  waiting for transfers between devices  437 us (40%)
  other arithmetic  61.7 us (6%)
  matrix products  40.3 us (4%)
  local copies, waits for them, and re-layouts  33.5 us (3%)
  between operations  14.8 us (1%)
    reduce_scatter x3, waiting for transfers between devices, per_device(): lax.psum_scatter(project_product.reshape(row_share * lax.axis_size('tp'),...  250 us
    reduce_scatter x3, waiting for transfers between devices, per_device(): lax.psum_scatter(contract_product.reshape(row_share * lax.axis_size('tp')...  187 us
    all_gather x3, blocking collectives, per_device(): row_piece = lax.all_gather(normed, 'tp', axis=0, tiled=True)  147 us
    all_gather x3, blocking collectives, per_device(): expand_row_piece = lax.all_gather(normed, 'tp', axis=0, tiled=True)  138 us
    all_gather x3, blocking collectives, carried_in(): pieces = lax.all_gather(value, axis)  134 us
    psum x1, blocking collectives, spread_2(): return lax.psum(jnp.where(mine, value, jnp.zeros_like(value)), axis)  79.2 us
    select_n x93, other arithmetic, step(): return jnp.where(position < mine, longer, so_far)  41.2 us
  transfers between devices with their start and end apart: 6, of which 6 were waited for; matrix products, arithmetic and copies ran while one was open for 0% of the time, Pallas kernels for 0%

commit v1 on v0

v1 whole, which is shorter than its diff:
```python
import functools

import jax
import jax.numpy as jnp
from jax import lax
from jax.experimental import pallas as pl
from jax.experimental.pallas import tpu as pltpu
from jax.sharding import PartitionSpec as P

ROUNDS = 3
EPSILON = 1e-06
MESH = pl.DeviceIdType.MESH
F32 = jnp.float32
BF16 = jnp.bfloat16

CHUNKS = 12
CHUNK = 192
PIECE = 48
HEAD_ROWS, WO_AT, UP_AT, DOWN_AT, ALL_ROWS = 576, 576, 768, 1536, 2304


def nt(a, b):
    return lax.dot_general(a, b, (((1,), (1,)), ((), ())), preferred_element_type=F32)


def nn(a, b):
    return jnp.dot(a, b, preferred_element_type=F32)


def ln_mod(values, shift, scale):
    average = jnp.mean(values, axis=-1, keepdims=True)
    centered = values - average
    spread = jnp.mean(centered * centered, axis=-1, keepdims=True)
    return (centered * lax.rsqrt(spread + EPSILON) * (1.0 + scale) + shift).astype(BF16)


def ln_rows(source, target, shift, scale, rows):
    def block(i, carry):
        at = pl.ds(pl.multiple_of(i * 16, 16), 16)
        target[at, :] = ln_mod(source[at, :].astype(F32), shift, scale)
        return carry

    lax.fori_loop(0, rows // 16, block, 0, unroll=2)


def head_norm_t(values, gain):
    split = values.reshape(values.shape[0] // 64, 64, values.shape[1])
    square = jnp.mean(split * split, axis=1, keepdims=True)
    return split * lax.rsqrt(square + EPSILON) * gain[None]


def device(z, x, core, y):
    z, x, y = (z + 8) % 8, (x + 4) % 4, (y + 4) % 4
    return (((z % 4) * 4 + x) * 2 + core, y * 2 + z // 4)


def kernel(
    traj, mods, steps, ctx, pos, patch, heads, q_gain, k_gain, text, wo, up, down, final,
    out,
    WB, WOF, TT, POS, XIN, XR, TN, CKN, CVT, CSEND, CRECV, H, N, ACC, AB, RSS, RSB,
    TS, US, SX, TEI, SZT, SZE,
    local, zs, zr, xs, xr, cs, cr, wos, wor, wfs, wfr,
    exs, exr, gs, gr, txs, txr, ats, atr, rss, rsr, us, ur, sxs, sxr, szs, szr,
):
    tm, tp = lax.axis_index("tm"), lax.axis_index("tp")
    zl, x, core = tm // 8, (tm // 2) % 4, tm % 2
    y, zh = tp // 2, tp % 2
    z = zh * 4 + zl
    way = 1 - 2 * core

    def copy(src, dst, send, recv, to):
        return pltpu.make_async_remote_copy(
            src_ref=src, dst_ref=dst, send_sem=send, recv_sem=recv, device_id=to, device_id_type=MESH
        )

    y_peers = [device(z, x, core, y + k) for k in (1, 2, 3)]
    x_peers = [device(z, x + k, core, y) for k in (1, 2, 3)]
    z_peers = [device(z + k, x, core, y) for k in range(1, 8)]
    other_core = device(z, x, 1 - core, y)
    other_half = device(z + 4, x, core, y)

    loads = [
        pltpu.make_async_copy(heads, WB.at[0, pl.ds(0, HEAD_ROWS)], local.at[0]),
        pltpu.make_async_copy(wo, WB.at[0, pl.ds(WO_AT, 192)], local.at[1]),
        pltpu.make_async_copy(
            up.at[pl.ds(0, 768)], WB.at[0, pl.ds(UP_AT, 768), pl.ds(0, 768)], local.at[2]
        ),
        pltpu.make_async_copy(
            up.at[pl.ds(768, 768)], WB.at[0, pl.ds(UP_AT, 768), pl.ds(768, 768)], local.at[3]
        ),
        pltpu.make_async_copy(down, WB.at[0, pl.ds(DOWN_AT, 768)], local.at[4]),
        pltpu.make_async_copy(text, TT, local.at[5]),
        pltpu.make_async_copy(wo, WOF.at[y, 0], local.at[6]),
    ]
    for load in loads:
        load.start()

    barrier = pltpu.get_barrier_semaphore()
    everyone = y_peers + x_peers + z_peers + [other_core]
    for peer in everyone:
        pl.semaphore_signal(barrier, inc=1, device_id=peer, device_id_type=MESH)
    pl.semaphore_wait(barrier, len(everyone))

    half = pl.ds(pl.multiple_of(zh * 16, 16), 16)
    ex_x = copy(traj.at[1 - zh], XR.at[zh], exs.at[0], exr.at[0], other_half)
    ex_pos = copy(pos, POS.at[y, half], exs.at[1], exr.at[1], other_half)
    ex_x.start()
    ex_pos.start()
    XR[zh] = traj[zh]
    POS[y, half, :] = pos[...]

    even = x % 2
    first = jnp.where(core == 0, zl == 3, zl == 0)
    own = 1 - first.astype(jnp.int32)
    z_quarter = 2 * core + even
    x_quarter = 2 * core + 1 - even

    def rows(quarter, c):
        return pl.ds(pl.multiple_of(c * CHUNK + quarter * PIECE, 16), PIECE)

    def z_copy(c):
        at = rows(z_quarter, c)
        return copy(
            WB.at[own, at], WB.at[1, at], zs.at[c], zr.at[c], device(z + way, x, core, y)
        )

    def x_copy(c):
        at = rows(z_quarter, c)
        return copy(WB.at[1, at], WB.at[1, at], xs.at[c], xr.at[c], device(z, x + way, core, y))

    def core_copy(k, quarter, c):
        at = rows(quarter, c)
        return copy(WB.at[1, at], WB.at[1, at], cs.at[k, c], cr.at[k, c], other_core)

    for load in loads[:5]:
        load.wait()

    @pl.when(first)
    def _():
        def send(c, carry):
            z_copy(c).start()
            return carry

        lax.fori_loop(0, CHUNKS, send, 0)

    def pump_x(c):
        x_copy(c).wait_recv()
        core_copy(1, x_quarter, c).start()

    def pump(c, carry):
        z_copy(c).wait_recv()

        @pl.when(jnp.logical_not(first))
        def _():
            z_copy(c).start()

        x_copy(c).start()
        core_copy(0, z_quarter, c).start()

        @pl.when(c > 0)
        def _():
            pump_x(c - 1)

        return carry

    def arrive(c, carry):
        core_copy(0, z_quarter, c).wait_recv()
        core_copy(1, x_quarter, c).wait_recv()
        return carry

    mine = pl.ds(pl.multiple_of(core * 96, 16), 96)

    def wo_copies(part):
        return [
            copy(
                WB.at[part, pl.ds(pl.multiple_of(WO_AT + core * 96, 16), 96)],
                WOF.at[y, part, mine],
                wos.at[part, k],
                wor.at[part, k],
                y_peers[k],
            )
            for k in range(3)
        ]

    def wo_forwards(part):
        return [
            copy(
                WOF.at[(y + 3 - k) % 4, part, mine],
                WOF.at[(y + 3 - k) % 4, part, mine],
                wfs.at[part, k],
                wfr.at[part, k],
                other_core,
            )
            for k in range(3)
        ]

    ex_x.wait()
    ex_pos.wait()
    XIN[0, y, 0:16, :] = XR[0].astype(BF16)
    XIN[0, y, 16:32, :] = XR[1].astype(BF16)

    def state_copies(r):
        return [
            copy(XIN.at[r, y], XIN.at[r, y], gs.at[r, k], gr.at[r, k], y_peers[k])
            for k in range(3)
        ]

    pos_copies = [
        copy(POS.at[y], POS.at[y], gs.at[3, k], gr.at[3, k], y_peers[k]) for k in range(3)
    ]
    for one in state_copies(0) + pos_copies:
        one.start()
    for one in wo_copies(0):
        one.start()

    pump(0, 0)

    loads[5].wait()
    loads[6].wait()

    def prompt(slot):
        ln_rows(ctx, TN, mods[slot, 6:7, :], mods[slot, 7:8, :], 128)
        joint = nt(TT[...], TN[...])
        keys = head_norm_t(joint[:192], k_gain[...]).reshape(192, 128)
        return keys, joint[192:].astype(BF16)

    keys, values = prompt(1 - zh)
    CSEND[0:192, :] = keys.astype(BF16)
    CSEND[192:384, :] = values
    text_copy = copy(CSEND, CRECV, txs, txr, other_half)
    text_copy.start()
    pump(1, 0)
    keys, values = prompt(zh)
    for i in range(3):
        CKN[0, i] = keys[i * 64 : (i + 1) * 64].T.astype(BF16)
    CVT[0] = values
    pump(2, 0)

    hop = jnp.where(core == 0, zl + 1, 4 - zl)
    before = jnp.where(hop == 1, 12, jnp.where(hop == 2, 10, jnp.where(hop == 3, 7, 5)))
    lax.fori_loop(3, before, pump, 0)

    text_copy.wait()
    for i in range(3):
        CKN[1, i] = CRECV[i * 64 : (i + 1) * 64, :].astype(F32).T.astype(BF16)
    CVT[1] = CRECV[192:384, :]
    for one in state_copies(0) + pos_copies:
        one.wait()
    lax.fori_loop(0, 3, arrive, 0)

    own_rows = pl.ds(pl.multiple_of(y * 32, 32), 32)
    start_slot = jnp.logical_and(tm == 0, zh == 0)

    def mod(k):
        return mods[zh, k : k + 1, :]

    def one_round(r, carry):
        X = XIN[r].reshape(128, 64)
        H[...] = nn(X, patch[...]) + POS[...].reshape(128, 1536).astype(F32)
        ln_rows(H, N, mod(0), mod(1), 128)

        parts = []
        for s in range(2):
            joint = nt(WB[s, 0:HEAD_ROWS, :], N[...])
            query = head_norm_t(joint[:192], q_gain[...]).astype(BF16)
            keys = head_norm_t(joint[192:384], k_gain[...])
            values = joint[384:].astype(BF16)
            for i in range(3):
                key_rows = jnp.concatenate([keys[i].T.astype(BF16), CKN[s, i]], axis=0)
                scores = nn(key_rows, query[i]) * 0.125
                powers = jnp.exp(scores)
                probs = (powers / jnp.sum(powers, axis=0, keepdims=True)).astype(BF16)
                both = jnp.concatenate(
                    [values[i * 64 : (i + 1) * 64], CVT[s, i * 64 : (i + 1) * 64, :]], axis=1
                )
                parts.append(nn(both, probs))
        AB[r, y] = jnp.concatenate(parts, axis=0).T.astype(BF16)
        attended = [
            copy(AB.at[r, y], AB.at[r, y], ats.at[r, k], atr.at[r, k], y_peers[k])
            for k in range(3)
        ]
        for one in attended:
            one.start()

        @pl.when(r == 0)
        def _():
            for one, forward in zip(wo_copies(0), wo_forwards(0)):
                one.wait_recv()
                forward.start()
            lax.fori_loop(before, CHUNKS, pump, 0)
            pump_x(CHUNKS - 1)
            for one in wo_copies(1):
                one.start()
            lax.fori_loop(3, CHUNKS, arrive, 0)
            fill = pltpu.make_async_copy(
                WB.at[1, pl.ds(WO_AT, 192)], WOF.at[y, 1], local.at[7]
            )
            fill.start()
            for one, forward in zip(wo_copies(1), wo_forwards(1)):
                one.wait_recv()
                forward.start()
            fill.wait()
            for part in range(2):
                for forward in wo_forwards(part):
                    forward.wait_recv()

        def project(k):
            return nn(AB[r, (y + k) % 4], WOF[(y + k) % 4].reshape(384, 1536))

        ACC[...] = project(0)
        for k, one in ((1, attended[2]), (3, attended[0]), (2, attended[1])):
            one.wait_recv()
            ACC[...] += project(k)
        H[...] = H[...] + mod(2) * ACC[...]
        ln_rows(H, N, mod(3), mod(4), 128)

        total = None
        for s in range(2):
            hidden = nn(N[:, 0:768], WB[s, UP_AT:DOWN_AT, 0:768]) + nn(
                N[:, 768:1536], WB[s, UP_AT:DOWN_AT, 768:1536]
            )
            active = jax.nn.gelu(hidden, approximate=True).astype(BF16)
            part = nn(active, WB[s, DOWN_AT:ALL_ROWS, :])
            total = part if total is None else total + part
        ACC[...] = total
        RSS[...] = total.astype(BF16)
        summed = [
            copy(
                RSS.at[pl.ds(pl.multiple_of(((y + k + 1) % 4) * 32, 32), 32)],
                RSB.at[r, k],
                rss.at[r, k],
                rsr.at[r, k],
                y_peers[k],
            )
            for k in range(3)
        ]
        for one in summed:
            one.start()
        for one in summed:
            one.wait_recv()
        contract = ACC[own_rows, :]
        for k in range(3):
            contract = contract + RSB[r, k].astype(F32)
        state = ln_mod(H[own_rows, :] + mod(5) * contract, mod(8), mod(9))
        term = steps[zh] * nt(state, final[...])
        anchor = jnp.concatenate([XR[0], XR[1]], axis=0)
        term = term - jnp.where(start_slot, anchor, jnp.zeros_like(anchor))

        TS[r] = term
        pair = copy(TS.at[r], US.at[r], us.at[r], ur.at[r], other_core)
        pair.start()
        pair.wait_recv()
        chip = term + US[r]
        SX[r, x] = chip
        along_x = [
            copy(SX.at[r, x], SX.at[r, x], sxs.at[r, k], sxr.at[r, k], x_peers[k])
            for k in range(3)
        ]
        for one in along_x:
            one.start()
        for one in along_x:
            one.wait_recv()
        before_me = jnp.where(core == 1, US[r], jnp.zeros_like(term))
        whole = jnp.zeros_like(term)
        for i in range(4):
            block = SX[r, i]
            whole = whole + block
            before_me = before_me + jnp.where(i < x, block, jnp.zeros_like(block))
        TEI[r, 0] = whole
        TEI[r, 1] = before_me
        TEI[r, 2] = before_me + term
        SZT[r, z] = whole
        along_z = [
            copy(TEI.at[r, pl.ds(1, 2)], SZE.at[r], szs.at[r, 7], szr.at[r, 7], other_half)
        ] + [
            copy(TEI.at[r, 0], SZT.at[r, z], szs.at[r, k - 1], szr.at[r, k - 1], z_peers[k - 1])
            for k in (4, 3, 5, 2, 6, 1, 7)
        ]
        for one in along_z:
            one.start()
        for one in along_z:
            one.wait_recv()
        base = jnp.zeros_like(term)
        for i in range(8):
            block = SZT[r, i]
            base = base + jnp.where(i % 4 < zl, block, jnp.zeros_like(block))
        upper = zh == 1
        earlier = base + before_me + jnp.where(upper, SZE[r, 1], SZE[r, 0])

        @pl.when(r < ROUNDS - 1)
        def _():
            fresh = jnp.where(start_slot, anchor, -earlier)
            XIN[r + 1, y] = fresh.astype(BF16)
            for one in state_copies(r + 1):
                one.start()
            for one in state_copies(r + 1):
                one.wait()

        @pl.when(r == ROUNDS - 1)
        def _():
            ACC[0:32, 0:64] = -(earlier + term)
            ACC[32:64, 0:64] = -(
                base + SZE[r, 1] + jnp.where(upper, before_me, before_me + term)
            )
            out[zh] = ACC[half, 0:64]
            out[1 - zh] = ACC[pl.ds(pl.multiple_of(32 + zh * 16, 16), 16), 0:64]

        for one in attended + summed + [pair] + along_x + along_z:
            one.wait_send()
        return carry

    lax.fori_loop(0, ROUNDS, one_round, 0)

    def drain(c, carry):
        z_copy(c).wait_send()
        x_copy(c).wait_send()
        core_copy(0, z_quarter, c).wait_send()
        core_copy(1, x_quarter, c).wait_send()
        return carry

    lax.fori_loop(0, CHUNKS, drain, 0)
    for part in range(2):
        for one in wo_copies(part) + wo_forwards(part):
            one.wait_send()


def per_device(
    trajectory,
    window_start,
    step_sizes,
    modulation,
    context,
    position_embed,
    patch_weight,
    heads_weight,
    query_gain,
    key_gain,
    text_weight,
    output_weight,
    up_weight,
    down_weight,
    final_weight,
):
    entry = window_start[0] + lax.axis_index("tm") * 2
    table = lax.dynamic_slice_in_dim(modulation, entry, 2).astype(F32)
    steps = lax.dynamic_slice_in_dim(step_sizes, entry, 2)
    steps = jnp.broadcast_to(steps[:, None, None], (2, 1, 64))
    heads = heads_weight.transpose(1, 2, 0).reshape(HEAD_ROWS, 1536)
    text = text_weight.transpose(1, 2, 0).reshape(384, 1536)
    vmem = pl.BlockSpec(memory_space=pltpu.VMEM)
    hbm = pl.BlockSpec(memory_space=pl.ANY)
    dma = pltpu.SemaphoreType.DMA
    R = ROUNDS
    return pl.pallas_call(
        kernel,
        out_shape=jax.ShapeDtypeStruct((2, 16, 64), F32),
        in_specs=[vmem] * 6 + [hbm, vmem, vmem, hbm, hbm, hbm, hbm, vmem],
        out_specs=vmem,
        scratch_shapes=[
            pltpu.VMEM((2, ALL_ROWS, 1536), BF16),
            pltpu.VMEM((4, 2, 192, 1536), BF16),
            pltpu.VMEM((384, 1536), BF16),
            pltpu.VMEM((4, 32, 1536), BF16),
            pltpu.VMEM((R, 4, 32, 64), BF16),
            pltpu.VMEM((2, 16, 64), F32),
            pltpu.VMEM((128, 1536), BF16),
            pltpu.VMEM((2, 3, 128, 64), BF16),
            pltpu.VMEM((2, 192, 128), BF16),
            pltpu.VMEM((384, 128), BF16),
            pltpu.VMEM((384, 128), BF16),
            pltpu.VMEM((128, 1536), F32),
            pltpu.VMEM((128, 1536), BF16),
            pltpu.VMEM((128, 1536), F32),
            pltpu.VMEM((R, 4, 128, 384), BF16),
            pltpu.VMEM((128, 1536), BF16),
            pltpu.VMEM((R, 3, 32, 1536), BF16),
            pltpu.VMEM((R, 32, 64), F32),
            pltpu.VMEM((R, 32, 64), F32),
            pltpu.VMEM((R, 4, 32, 64), F32),
            pltpu.VMEM((R, 3, 32, 64), F32),
            pltpu.VMEM((R, 8, 32, 64), F32),
            pltpu.VMEM((R, 2, 32, 64), F32),
            dma((8,)),
            dma((CHUNKS,)),
            dma((CHUNKS,)),
            dma((CHUNKS,)),
            dma((CHUNKS,)),
            dma((2, CHUNKS)),
            dma((2, CHUNKS)),
            dma((2, 3)),
            dma((2, 3)),
            dma((2, 3)),
            dma((2, 3)),
            dma((2,)),
            dma((2,)),
            dma((4, 3)),
            dma((4, 3)),
            dma,
            dma,
            dma((R, 3)),
            dma((R, 3)),
            dma((R, 3)),
            dma((R, 3)),
            dma((R,)),
            dma((R,)),
            dma((R, 3)),
            dma((R, 3)),
            dma((R, 8)),
            dma((R, 8)),
        ],
        compiler_params=pltpu.CompilerParams(
            collective_id=0, has_side_effects=True, vmem_limit_bytes=56 << 20
        ),
        cost_estimate=pl.CostEstimate(
            flops=7_000_000_000, bytes_accessed=10_000_000, transcendentals=1_000_000
        ),
        name="picard",
    )(
        trajectory,
        table,
        steps,
        context,
        position_embed,
        patch_weight,
        heads,
        query_gain[:, None],
        key_gain[:, None],
        text,
        output_weight,
        up_weight,
        down_weight,
        final_weight.T,
    )


def solution(mesh):
    return jax.shard_map(
        per_device,
        mesh=mesh,
        in_specs=(
            P("tm", "tp", None),
            P(),
            P(),
            P(),
            P(),
            P("tp", None),
            P(),
            P(None, None, "tp"),
            P(),
            P(),
            P(None, None, "tp"),
            P("tp", None),
            P(None, "tp"),
            P("tp", None),
            P(),
        ),
        out_specs=P("tm", "tp", None),
        check_vma=False,
    )
```

time: 1090 us -> 175 us (0.16)
  blocking collectives: 497 us -> 0 us
  waiting for transfers between devices: 437 us -> 0 us
  Pallas kernels: 0 us -> 167 us
  other arithmetic: 61.7 us -> 0.69 us
  matrix products: 40.3 us -> 0 us
  local copies, waits for them, and re-layouts: 33.5 us -> 6.67 us
  between operations: 14.8 us -> 0.82 us
    reduce_scatter x6 -> x0, waiting for transfers between devices: 437 us -> none  [the longest x3 250 us: per_device(): lax.psum_scatter(project_product.reshape(row_share * lax.axis_size('tp'),...]
    all_gather x9 -> x0, blocking collectives: 418 us -> none  [the longest x3 147 us: per_device(): row_piece = lax.all_gather(normed, 'tp', axis=0, tiled=True)]
    pallas_call x0 -> x1, Pallas kernels: none -> 167 us  [per_device(): pl.pallas_call(kernel, out_shape=jax.ShapeDtypeStruct((2, 16, 64), F32),...]
    psum x1 -> x0, blocking collectives: 79.2 us -> none  [spread_2(): return lax.psum(jnp.where(mine, value, jnp.zeros_like(value)), axis)]
    select_n x94 -> x0, other arithmetic: 41.2 us -> none  [the longest x93 41.2 us: step(): return jnp.where(position < mine, longer, so_far)]
    dot_general x22 -> x0, matrix products: 40.3 us -> none  [the longest x3 13.7 us: per_device(): jnp.dot(activated.reshape(-1, activated.shape[2]), down_weight, preferred...]
    convert_element_type x6 -> x0, local copies, waits for them, and re-layouts: 15 us -> none  [per_device(): hidden = hidden + slot_table[:, :, 5] * lax.psum_scatter(contract_product...]
    reduce_sum x24 -> x0, other arithmetic: 11.5 us -> none  [the longest x7 6.12 us: layer_norm(): average = jnp.mean(values, axis=-1, keepdims=True)]
  transfers between devices with their start and end apart: 6 -> 0, of which waited for: 6 -> 0; matrix products, arithmetic and copies ran while one was open for 0% -> 0% of each run, Pallas kernels for 0% -> 0%
where the time goes in v1:
time: 175 us
  Pallas kernels  167 us (95%)
  local copies, waits for them, and re-layouts  6.67 us (4%)
    pallas_call x1, Pallas kernels, per_device(): pl.pallas_call(kernel, out_shape=jax.ShapeDtypeStruct((2, 16, 64), F32),...  167 us

profile of v1, /device:TPU:1, one launch (start us, length us, event | category | flops | bytes accessed | tf_op | source)
XLA Modules:
  0.0 174.8 jit_solution(1224609351910862452)
XLA Ops:
  0.0 0.0 copy-start
  0.8 1.2 copy-done
  2.0 0.1 constant_dynamic-slice_fusion
  2.1 0.7 copy_convert_fusion.mods
  2.8 0.7 dynamic_slice.7
  3.5 0.6 broadcast_in_dim.12.steps
  4.1 1.4 copy.17.q_gain
  5.5 1.4 copy.18.k_gain
  6.8 166.6 %picard.1 = f32[2,16,64]{2,1,0:T(8,128)} custom-call(f32[2,16,64]{2,1,0:T(8,128)} %traj.1, f32[2,10,1536]{2,1,0:T(8,128)} %copy_convert_fusion.mods, f32[2,1,64]{2,1,0:T(1,128)} %broadcast_in_dim.12.steps, bf16[128,1536]{1,0:T(8,128)(2,1)} %ctx.1, bf16[16,1536]{1,0:T(8,128)(2,1)} %pos.1, bf16[64,1536]{1,0:T(8,128)(2,1)} %patch.1, ...), custom_call_target="tpu_custom_call" | custom-call | flops 7000000000 | bytes 10000000 | tf_op jit(solution)/shard_map/picard/pallas_call | solution.py:454
  173.5 1.3 copy.23
Async XLA Ops:
  0.0 2.0 %copy-start = (bf16[112,10,1536]{2,0,1:T(8,128)(2,1)S(1)}, bf16[112,10,1536]{2,0,1:T(8,128)(2,1)}, u32[]{:S(2)}) copy-start(bf16[112,10,1536]{2,0,1:T(8,128)(2,1)} %param.18) | copy-start | bytes 10321924

commit v2 on v1

v2 whole, which is shorter than its diff:
```python
import functools

import jax
import jax.numpy as jnp
from jax import lax
from jax.experimental import pallas as pl
from jax.experimental.pallas import tpu as pltpu
from jax.sharding import PartitionSpec as P

ROUNDS = 3
EPSILON = 1e-06
MESH = pl.DeviceIdType.MESH
F32 = jnp.float32
BF16 = jnp.bfloat16

LAG = 3
CHUNKS = 12
CHUNK = 192
STEPS = CHUNKS + LAG
PIECE = 48
HEAD_ROWS = 576
WO_AT, HEADS_AT, UP_AT, DOWN_AT, ALL_ROWS = 0, 192, 768, 1536, 2304


def nt(a, b):
    return lax.dot_general(a, b, (((1,), (1,)), ((), ())), preferred_element_type=F32)


def nn(a, b):
    return jnp.dot(a, b, preferred_element_type=F32)


def ln_mod(values, shift, scale):
    average = jnp.mean(values, axis=-1, keepdims=True)
    centered = values - average
    spread = jnp.mean(centered * centered, axis=-1, keepdims=True)
    return (centered * lax.rsqrt(spread + EPSILON) * (1.0 + scale) + shift).astype(BF16)


def ln_rows(source, target, shift, scale, start, rows):
    def block(i, carry):
        at = pl.ds(pl.multiple_of(start + i * 16, 16), 16)
        target[at, :] = ln_mod(source[at, :].astype(F32), shift, scale)
        return carry

    lax.fori_loop(0, rows // 16, block, 0, unroll=2)


def head_norm_t(values, gain):
    split = values.reshape(values.shape[0] // 64, 64, values.shape[1])
    square = jnp.mean(split * split, axis=1, keepdims=True)
    return split * lax.rsqrt(square + EPSILON) * gain[None]


def device(z, x, core, y):
    z, x, y = (z + 8) % 8, (x + 4) % 4, (y + 4) % 4
    return (((z % 4) * 4 + x) * 2 + core, y * 2 + z // 4)


def kernel(
    traj, start, steps, table, ctx, pos, patch, heads, q_gain, k_gain, text, wo, up, down, final,
    out,
    WB, WOF, TT, POS, XIN, XR, TN, CKN, CVT, CS, CRECV, H, N, ACC, AB, RSS, RSB,
    TZ, SUMS, XS, TABLE, MODS, CTX, PATCH, FINAL, GAINS,
    local, zs, zr, xs, xr, cs, cr, wos, wor, wfs, wfr,
    exs, exr, gs, gr, txs, txr, ats, atr, rss, rsr, sxs, sxr, szs, szr,
):
    tm, tp = lax.axis_index("tm"), lax.axis_index("tp")
    zl, x, core = tm // 8, (tm // 2) % 4, tm % 2
    y, zh = tp // 2, tp % 2
    z = zh * 4 + zl
    way = 1 - 2 * core

    def copy(src, dst, send, recv, to):
        return pltpu.make_async_remote_copy(
            src_ref=src, dst_ref=dst, send_sem=send, recv_sem=recv, device_id=to, device_id_type=MESH
        )

    y_peers = [device(z, x, core, y + k) for k in (1, 2, 3)]
    z_peers = [device(z + k, x, core, y) for k in range(1, 8)]
    other_core = device(z, x, 1 - core, y)
    other_half = device(z + 4, x, core, y)

    barrier = pltpu.get_barrier_semaphore()
    x_peers = [device(z, x + k // 2, (core + k) % 2, y) for k in range(1, 8)]
    everyone = y_peers + x_peers + z_peers
    for peer in everyone:
        pl.semaphore_signal(barrier, inc=1, device_id=peer, device_id_type=MESH)

    loads = [
        pltpu.make_async_copy(src, dst, local.at[i])
        for i, (src, dst) in enumerate(
            [
                (wo, WB.at[0, pl.ds(WO_AT, 192)]),
                (heads, WB.at[0, pl.ds(HEADS_AT, HEAD_ROWS)]),
                (up.at[pl.ds(0, 768)], WB.at[0, pl.ds(UP_AT, 768), pl.ds(0, 768)]),
                (up.at[pl.ds(768, 768)], WB.at[0, pl.ds(UP_AT, 768), pl.ds(768, 768)]),
                (down, WB.at[0, pl.ds(DOWN_AT, 768)]),
                (table, TABLE),
                (ctx, CTX),
                (text, TT),
                (patch, PATCH),
                (wo, WOF.at[y, 0]),
                (final, FINAL),
            ]
        )
    ]
    for i in (5, 0, 1, 2, 3, 4, 6, 7, 8, 9, 10):
        loads[i].start()

    entry = start[0] + tm * 2
    line = lax.broadcasted_iota(jnp.int32, (8, 112), 0)
    wanted = entry + jnp.where(line == 0, zh, 1 - zh)
    pick = (lax.broadcasted_iota(jnp.int32, (8, 112), 1) == wanted).astype(F32)
    step = jnp.sum(pick[0:1] * steps[...], axis=1, keepdims=True)
    pick = pick.astype(BF16)
    loads[5].wait()
    for k in range(10):
        MODS[k] = nn(pick, TABLE[k])
    GAINS[0] = jnp.broadcast_to(q_gain[...], (128, 64)).T
    GAINS[1] = jnp.broadcast_to(k_gain[...], (128, 64)).T

    pl.semaphore_wait(barrier, len(everyone))

    half = pl.ds(pl.multiple_of(zh * 16, 16), 16)
    ex_x = copy(traj.at[1 - zh], XR.at[zh], exs.at[0], exr.at[0], other_half)
    ex_pos = copy(pos, POS.at[y, half], exs.at[1], exr.at[1], other_half)
    ex_x.start()
    ex_pos.start()
    XR[zh] = traj[zh]
    POS[y, half, :] = pos[...]

    even = x % 2
    first = jnp.where(core == 0, zl == 3, zl == 0)
    own = 1 - first.astype(jnp.int32)
    z_quarter = 2 * core + even

    def rows(quarter, c):
        return pl.ds(pl.multiple_of(c * CHUNK + quarter * PIECE, 16), PIECE)

    def z_copy(c):
        at = rows(z_quarter, c)
        return copy(
            WB.at[own, at], WB.at[1, at], zs.at[c], zr.at[c], device(z + way, x, core, y)
        )

    def x_copy(c):
        at = rows(z_quarter, c)
        return copy(WB.at[1, at], WB.at[1, at], xs.at[c], xr.at[c], device(z, x + way, core, y))

    def core_copy(c):
        at = pl.ds(pl.multiple_of(c * CHUNK + core * 2 * PIECE, 16), 2 * PIECE)
        return copy(WB.at[1, at], WB.at[1, at], cs.at[c], cr.at[c], other_core)

    for load in loads[0:5]:
        load.wait()

    @pl.when(first)
    def _():
        def send(c, carry):
            z_copy(c).start()
            return carry

        lax.fori_loop(0, CHUNKS, send, 0)

    def pump_x(c):
        x_copy(c).wait_recv()
        core_copy(c).start()

    def pump(c, carry):
        @pl.when(c < CHUNKS)
        def _():
            z_copy(c).wait_recv()

            @pl.when(jnp.logical_not(first))
            def _():
                z_copy(c).start()

            x_copy(c).start()

        @pl.when(c >= LAG)
        def _():
            pump_x(c - LAG)

        @pl.when(c == LAG)
        def _():
            for one in wo_copies(1):
                one.start()

        return carry

    def arrive(c, carry):
        core_copy(c).wait_recv()
        return carry

    mine = pl.ds(pl.multiple_of(core * 96, 16), 96)

    def wo_copies(part):
        return [
            copy(
                WB.at[part, pl.ds(pl.multiple_of(WO_AT + core * 96, 16), 96)],
                WOF.at[y, part, mine],
                wos.at[part, k],
                wor.at[part, k],
                y_peers[k],
            )
            for k in range(3)
        ]

    def wo_forwards(part):
        return [
            copy(
                WOF.at[(y + 3 - k) % 4, part, mine],
                WOF.at[(y + 3 - k) % 4, part, mine],
                wfs.at[part, k],
                wfr.at[part, k],
                other_core,
            )
            for k in range(3)
        ]

    loads[6].wait()
    loads[7].wait()
    text_copy = copy(CS.at[1 - zh], CRECV, txs, txr, other_half)

    def prompt(c):
        of_other = c < 6
        slot = jnp.where(of_other, 1 - zh, zh)
        part = c % 6

        @pl.when(part < 4)
        def _():
            shift, scale = (
                jnp.where(of_other, MODS[k, 1:2, :], MODS[k, 0:1, :]) for k in (6, 7)
            )
            ln_rows(CTX, TN, shift, scale, part * 32, 32)

        @pl.when(part == 4)
        def _():
            keys = head_norm_t(nt(TT[0:192, :], TN[...]), GAINS[1])
            CS[slot, 0:192, :] = keys.reshape(192, 128).astype(BF16)

        @pl.when(part == 5)
        def _():
            CS[slot, 192:384, :] = nt(TT[192:384, :], TN[...]).astype(BF16)

        @pl.when(c == 5)
        def _():
            text_copy.start()

    def only_prompt(c, carry):
        prompt(c)
        return carry

    hop = jnp.where(core == 0, zl + 1, 4 - zl)

    def by_hop(*values):
        return jnp.where(
            hop == 1,
            values[0],
            jnp.where(hop == 2, values[1], jnp.where(hop == 3, values[2], values[3])),
        )

    ready, before, middle = by_hop(0, 6, 12, 12), by_hop(15, 14, 9, 7), by_hop(15, 15, 15, 10)
    lax.fori_loop(0, ready, only_prompt, 0)
    pump(0, 0)

    ex_x.wait()
    ex_pos.wait()
    anchor = jnp.concatenate([XR[0], XR[1]], axis=1)
    XIN[0, y] = anchor.astype(BF16)

    def state_copies(r):
        return [
            copy(XIN.at[r, y], XIN.at[r, y], gs.at[r, k], gr.at[r, k], y_peers[k])
            for k in range(3)
        ]

    pos_copies = [
        copy(POS.at[y], POS.at[y], gs.at[3, k], gr.at[3, k], y_peers[k]) for k in range(3)
    ]
    for one in state_copies(0) + pos_copies:
        one.start()
    for one in wo_copies(0):
        one.start()

    def pump_prompt(c, carry):
        pump(c, carry)

        @pl.when(ready + c - 1 < 12)
        def _():
            prompt(ready + c - 1)

        return carry

    lax.fori_loop(1, before, pump_prompt, 0)
    lax.fori_loop(jnp.minimum(ready + before - 1, 12), 12, only_prompt, 0)
    loads[8].wait()
    loads[9].wait()
    loads[10].wait()
    for one in state_copies(0) + pos_copies:
        one.wait()

    own_rows = pl.ds(pl.multiple_of(y * 32, 32), 32)
    start_slot = jnp.logical_and(tm == 0, zh == 0)

    def mod(k):
        return MODS[k, 0:1, :]

    def one_round(r, carry):
        halves = XIN[r].astype(F32)
        X = jnp.concatenate(
            [halves[i // 2, :, 64 * (i % 2) : 64 * (i % 2) + 64] for i in range(8)], axis=0
        ).astype(BF16)
        H[...] = nn(X, PATCH[...]) + POS[...].reshape(128, 1536).astype(F32)
        ln_rows(H, N, mod(0), mod(1), 0, 128)

        @pl.when(r == 0)
        def _():
            text_copy.wait()
            for i in range(3):
                at = slice(i * 64, (i + 1) * 64)
                CKN[0, i] = CS[zh, at, :].astype(F32).T.astype(BF16)
                CKN[1, i] = CRECV[at, :].astype(F32).T.astype(BF16)
            CVT[0] = CS[zh, 192:384, :]
            CVT[1] = CRECV[192:384, :]
            lax.fori_loop(1, 4, arrive, 0)

        parts = []

        def head_copies(p):
            at = pl.ds(p * 128, 128)
            return [
                copy(
                    AB.at[r, y, :, at],
                    AB.at[r, y, :, at],
                    ats.at[r, p, k],
                    atr.at[r, p, k],
                    y_peers[k],
                )
                for k in range(3)
            ]

        def send_heads(p):
            AB[r, y, :, p * 128 : (p + 1) * 128] = jnp.concatenate(parts, axis=0).T.astype(BF16)
            for one in head_copies(p):
                one.start()
            parts.clear()

        attended = [head_copies(p) for p in range(3)]
        for s in range(2):
            joint = nt(WB[s, HEADS_AT:UP_AT, :], N[...])
            query = head_norm_t(joint[:192], GAINS[0]).astype(BF16)
            keys = head_norm_t(joint[192:384], GAINS[1])
            values = joint[384:].astype(BF16)
            for i in range(3):
                key_rows = jnp.concatenate([keys[i].T.astype(BF16), CKN[s, i]], axis=0)
                scores = nn(key_rows, query[i]) * 0.125
                powers = jnp.exp(scores)
                probs = (powers / jnp.sum(powers, axis=0, keepdims=True)).astype(BF16)
                both = jnp.concatenate(
                    [values[i * 64 : (i + 1) * 64], CVT[s, i * 64 : (i + 1) * 64, :]], axis=1
                )
                parts.append(nn(both, probs))
                if len(parts) == 2:
                    send_heads((3 * s + i) // 2)

        @pl.when(r == 0)
        def _():
            for one, forward in zip(wo_copies(0), wo_forwards(0)):
                one.wait_recv()
                forward.start()
            lax.fori_loop(before, middle, pump, 0)
            lax.fori_loop(0, 1, arrive, 0)
            fill = pltpu.make_async_copy(
                WB.at[1, pl.ds(WO_AT, 192)], WOF.at[y, 1], local.at[11]
            )
            fill.start()
            for one, forward in zip(wo_copies(1), wo_forwards(1)):
                one.wait_recv()
                forward.start()
            fill.wait()
            for part in range(2):
                for forward in wo_forwards(part):
                    forward.wait_recv()

        def project(k):
            return nn(AB[r, (y + k) % 4], WOF[(y + k) % 4].reshape(384, 1536))

        ACC[...] = project(0)
        for k, i in ((1, 2), (3, 0), (2, 1)):
            for p in range(3):
                attended[p][i].wait_recv()
            ACC[...] += project(k)
        H[...] = H[...] + mod(2) * ACC[...]
        ln_rows(H, N, mod(3), mod(4), 0, 128)

        @pl.when(r == 0)
        def _():
            lax.fori_loop(middle, STEPS, pump, 0)
            lax.fori_loop(4, 8, arrive, 0)

        active = []
        for s in range(2):
            hidden = nn(N[:, 0:768], WB[s, UP_AT:DOWN_AT, 0:768]) + nn(
                N[:, 768:1536], WB[s, UP_AT:DOWN_AT, 768:1536]
            )
            active.append(jax.nn.gelu(hidden, approximate=True).astype(BF16))

        @pl.when(r == 0)
        def _():
            lax.fori_loop(8, CHUNKS, arrive, 0)

        summed = []
        for p in range(2):
            at = slice(p * 768, (p + 1) * 768)
            total = nn(active[0], WB[0, DOWN_AT:ALL_ROWS, at]) + nn(
                active[1], WB[1, DOWN_AT:ALL_ROWS, at]
            )
            ACC[:, at] = total
            RSS[:, at] = total.astype(BF16)
            for k in range(3):
                one = copy(
                    RSS.at[
                        pl.ds(pl.multiple_of(((y + k + 1) % 4) * 32, 32), 32),
                        pl.ds(p * 768, 768),
                    ],
                    RSB.at[r, k, :, pl.ds(p * 768, 768)],
                    rss.at[r, p, k],
                    rsr.at[r, p, k],
                    y_peers[k],
                )
                one.start()
                summed.append(one)
        for one in summed:
            one.wait_recv()
        contract = ACC[own_rows, :]
        for k in range(3):
            contract = contract + RSB[r, k].astype(F32)
        state = ln_mod(H[own_rows, :] + mod(5) * contract, mod(8), mod(9))
        term = step * nt(state, FINAL[...])
        term = jnp.concatenate([term[0:16], term[16:32]], axis=1)
        anchor = jnp.concatenate([XR[0], XR[1]], axis=1)
        term = term - jnp.where(start_slot, anchor, jnp.zeros_like(anchor))

        TZ[r, z] = term
        along_z = [
            copy(TZ.at[r, z], TZ.at[r, z], szs.at[r, k - 1], szr.at[r, k - 1], z_peers[k - 1])
            for k in (4, 3, 5, 2, 6, 1, 7)
        ]
        for one in along_z:
            one.start()
        for one in along_z:
            one.wait_recv()
        lower = TZ[r, zl]
        both_halves = lower + TZ[r, zl + 4]
        below = jnp.zeros_like(term)
        for i in range(8):
            block = TZ[r, i]
            below = below + jnp.where(i % 4 < zl, block, jnp.zeros_like(block))
        SUMS[r, 0] = below
        SUMS[r, 1] = below + both_halves
        XS[r, x, core] = below
        along_x = []
        for k in range(1, 8):
            to_x, to_core = (x + k // 2) % 4, (core + k) % 2
            later = (2 * to_x + to_core > 2 * x + core).astype(jnp.int32)
            one = copy(
                SUMS.at[r, later],
                XS.at[r, x, core],
                sxs.at[r, k - 1],
                sxr.at[r, k - 1],
                device(z, to_x, to_core, y),
            )
            one.start()
            along_x.append(one)
        for one in along_x:
            one.wait_recv()
        base = jnp.zeros_like(term)
        for i in range(8):
            base = base + XS[r, i // 2, i % 2]
        upper = zh == 1

        @pl.when(r < ROUNDS - 1)
        def _():
            earlier = base + jnp.where(upper, lower, jnp.zeros_like(lower))
            XIN[r + 1, y] = jnp.where(start_slot, anchor, -earlier).astype(BF16)
            for one in state_copies(r + 1):
                one.start()
            for one in state_copies(r + 1):
                one.wait()

        @pl.when(r == ROUNDS - 1)
        def _():
            for s, total in enumerate([base + lower, base + both_halves]):
                out[s] = -jnp.where(upper, total[:, 64:128], total[:, 0:64])

        for one in sum(attended, []) + summed + along_x + along_z:
            one.wait_send()
        return carry

    lax.fori_loop(0, ROUNDS, one_round, 0)

    def drain(c, carry):
        z_copy(c).wait_send()
        x_copy(c).wait_send()
        core_copy(c).wait_send()
        return carry

    lax.fori_loop(0, CHUNKS, drain, 0)
    for part in range(2):
        for one in wo_copies(part) + wo_forwards(part):
            one.wait_send()


def per_device(
    trajectory,
    window_start,
    step_sizes,
    modulation,
    context,
    position_embed,
    patch_weight,
    heads_weight,
    query_gain,
    key_gain,
    text_weight,
    output_weight,
    up_weight,
    down_weight,
    final_weight,
):
    heads = heads_weight.transpose(1, 2, 0).reshape(HEAD_ROWS, 1536)
    text = text_weight.transpose(1, 2, 0).reshape(384, 1536)
    vmem = pl.BlockSpec(memory_space=pltpu.VMEM)
    hbm = pl.BlockSpec(memory_space=pl.ANY)
    dma = pltpu.SemaphoreType.DMA
    R = ROUNDS
    return pl.pallas_call(
        kernel,
        out_shape=jax.ShapeDtypeStruct((2, 16, 64), F32),
        in_specs=[vmem, pl.BlockSpec(memory_space=pltpu.SMEM), vmem, hbm, hbm, vmem, hbm, hbm]
        + [vmem, vmem, hbm, hbm, hbm, hbm, hbm],
        out_specs=vmem,
        scratch_shapes=[
            pltpu.VMEM((2, ALL_ROWS, 1536), BF16),
            pltpu.VMEM((4, 2, 192, 1536), BF16),
            pltpu.VMEM((384, 1536), BF16),
            pltpu.VMEM((4, 32, 1536), BF16),
            pltpu.VMEM((R, 4, 16, 128), BF16),
            pltpu.VMEM((2, 16, 64), F32),
            pltpu.VMEM((128, 1536), BF16),
            pltpu.VMEM((2, 3, 128, 64), BF16),
            pltpu.VMEM((2, 192, 128), BF16),
            pltpu.VMEM((2, 384, 128), BF16),
            pltpu.VMEM((384, 128), BF16),
            pltpu.VMEM((128, 1536), F32),
            pltpu.VMEM((128, 1536), BF16),
            pltpu.VMEM((128, 1536), F32),
            pltpu.VMEM((R, 4, 128, 384), BF16),
            pltpu.VMEM((128, 1536), BF16),
            pltpu.VMEM((R, 3, 32, 1536), BF16),
            pltpu.VMEM((R, 8, 16, 128), F32),
            pltpu.VMEM((R, 2, 16, 128), F32),
            pltpu.VMEM((R, 4, 2, 16, 128), F32),
            pltpu.VMEM((10, 112, 1536), BF16),
            pltpu.VMEM((10, 8, 1536), F32),
            pltpu.VMEM((128, 1536), BF16),
            pltpu.VMEM((64, 1536), BF16),
            pltpu.VMEM((64, 1536), BF16),
            pltpu.VMEM((2, 64, 128), F32),
            dma((12,)),
            dma((CHUNKS,)),
            dma((CHUNKS,)),
            dma((CHUNKS,)),
            dma((CHUNKS,)),
            dma((CHUNKS,)),
            dma((CHUNKS,)),
            dma((2, 3)),
            dma((2, 3)),
            dma((2, 3)),
            dma((2, 3)),
            dma((2,)),
            dma((2,)),
            dma((4, 3)),
            dma((4, 3)),
            dma,
            dma,
            dma((R, 3, 3)),
            dma((R, 3, 3)),
            dma((R, 2, 3)),
            dma((R, 2, 3)),
            dma((R, 7)),
            dma((R, 7)),
            dma((R, 7)),
            dma((R, 7)),
        ],
        compiler_params=pltpu.CompilerParams(
            collective_id=0, has_side_effects=True, vmem_limit_bytes=56 << 20
        ),
        cost_estimate=pl.CostEstimate(
            flops=7_000_000_000, bytes_accessed=10_000_000, transcendentals=1_000_000
        ),
        name="picard",
    )(
        trajectory,
        window_start,
        step_sizes[None],
        modulation.transpose(1, 0, 2),
        context,
        position_embed,
        patch_weight,
        heads,
        query_gain[None],
        key_gain[None],
        text,
        output_weight,
        up_weight,
        down_weight,
        final_weight.T,
    )


def solution(mesh):
    return jax.shard_map(
        per_device,
        mesh=mesh,
        in_specs=(
            P("tm", "tp", None),
            P(),
            P(),
            P(),
            P(),
            P("tp", None),
            P(),
            P(None, None, "tp"),
            P(),
            P(),
            P(None, None, "tp"),
            P("tp", None),
            P(None, "tp"),
            P("tp", None),
            P(),
        ),
        out_specs=P("tm", "tp", None),
        check_vma=False,
    )
```

time: 175 us -> 149 us (0.85)
  Pallas kernels: 167 us -> 147 us
  local copies, waits for them, and re-layouts: 6.67 us -> 1.32 us
    pallas_call x1, Pallas kernels: 167 us -> 147 us  [per_device(): pl.pallas_call(kernel, out_shape=jax.ShapeDtypeStruct((2, 16, 64), F32),...]
    broadcast_in_dim x3 -> x0, local copies, waits for them, and re-layouts: 3.34 us -> none  [the longest x1 1.36 us: per_device(): query_gain[:, None]]
where the time goes in v2:
time: 149 us
  Pallas kernels  147 us (99%)
    pallas_call x1, Pallas kernels, per_device(): pl.pallas_call(kernel, out_shape=jax.ShapeDtypeStruct((2, 16, 64), F32),...  147 us

profile of v2, /device:TPU:1, one launch (start us, length us, event | category | flops | bytes accessed | tf_op | source)
XLA Modules:
  0.0 148.8 jit_solution(17987746732877065747)
XLA Ops:
  0.7 146.8 %picard.1 = f32[2,16,64]{2,1,0:T(8,128)} custom-call(f32[2,16,64]{2,1,0:T(8,128)} %traj.1, s32[1]{0:T(128)S(6)} %copy.17.start, f32[1,112]{1,0:T(1,128)} %bitcast.15, bf16[10,112,1536]{2,1,0:T(8,128)(2,1)} %bitcast.11, bf16[128,1536]{1,0:T(8,128)(2,1)} %ctx.1, bf16[16,1536]{1,0:T(8,128)(2,1)} %pos.1, bf16[64,1536]{1,0:T(8,128)(2,1)} %patch.1, ...), custom_call_target="tpu_custom_call" | custom-call | flops 7000000000 | bytes 10000000 | tf_op jit(solution)/shard_map/picard/pallas_call | solution.py:539
  147.5 1.3 copy.18

commit v3 on v2

--- a/solution.py
+++ b/solution.py
@@ -14,12 +14,14 @@
 BF16 = jnp.bfloat16
 
 LAG = 3
-CHUNKS = 12
-CHUNK = 192
+CHUNKS = 18
+CHUNK = 128
 STEPS = CHUNKS + LAG
-PIECE = 48
+PIECE = 32
 HEAD_ROWS = 576
-WO_AT, HEADS_AT, UP_AT, DOWN_AT, ALL_ROWS = 0, 192, 768, 1536, 2304
+FAR_FIRST = (1, 0, 2)
+FIRST = 6
+HEADS_AT, WO_AT, UP_AT, DOWN_AT, ALL_ROWS = 0, 576, 768, 1536, 2304
 
 
 def nt(a, b):
@@ -43,7 +45,7 @@
         target[at, :] = ln_mod(source[at, :].astype(F32), shift, scale)
         return carry
 
-    lax.fori_loop(0, rows // 16, block, 0, unroll=2)
+    lax.fori_loop(0, rows // 16, block, 0, unroll=8 if rows == 128 else 2)
 
 
 def head_norm_t(values, gain):
@@ -63,7 +65,7 @@
     WB, WOF, TT, POS, XIN, XR, TN, CKN, CVT, CS, CRECV, H, N, ACC, AB, RSS, RSB,
     TZ, SUMS, XS, TABLE, MODS, CTX, PATCH, FINAL, GAINS,
     local, zs, zr, xs, xr, cs, cr, wos, wor, wfs, wfr,
-    exs, exr, gs, gr, txs, txr, ats, atr, rss, rsr, sxs, sxr, szs, szr,
+    exs, exr, gs, gr, txs, txr, ats, atr, rss, rsr, sxs, sxr, szs, szr, mxs, mxr,
 ):
     tm, tp = lax.axis_index("tm"), lax.axis_index("tp")
     zl, x, core = tm // 8, (tm // 2) % 4, tm % 2
@@ -105,8 +107,53 @@
             ]
         )
     ]
-    for i in (5, 0, 1, 2, 3, 4, 6, 7, 8, 9, 10):
+    for i in (1, 0, 5, 6, 7, 2, 3, 4, 8, 9, 10):
         loads[i].start()
+
+    pl.semaphore_wait(barrier, len(everyone))
+
+    half = pl.ds(pl.multiple_of(zh * 16, 16), 16)
+    ex_x = copy(traj.at[1 - zh], XR.at[zh], exs.at[0], exr.at[0], other_half)
+    ex_pos = copy(pos, POS.at[y, half], exs.at[1], exr.at[1], other_half)
+    ex_x.start()
+    ex_pos.start()
+    XR[zh] = traj[zh]
+    POS[y, half, :] = pos[...]
+
+    even = x % 2
+    first = jnp.where(core == 0, zl == 3, zl == 0)
+    own = 1 - first.astype(jnp.int32)
+    z_quarter = 2 * core + even
+
+    def rows(quarter, c):
+        return pl.ds(pl.multiple_of(c * CHUNK + quarter * PIECE, 16), PIECE)
+
+    def z_copy(c):
+        at = rows(z_quarter, c)
+        return copy(
+            WB.at[own, at], WB.at[1, at], zs.at[c], zr.at[c], device(z + way, x, core, y)
+        )
+
+    def x_copy(c):
+        at = rows(z_quarter, c)
+        return copy(WB.at[1, at], WB.at[1, at], xs.at[c], xr.at[c], device(z, x + way, core, y))
+
+    def core_copy(c):
+        at = pl.ds(pl.multiple_of(c * CHUNK + core * 2 * PIECE, 16), 2 * PIECE)
+        return copy(WB.at[1, at], WB.at[1, at], cs.at[c], cr.at[c], other_core)
+
+    def send_own(low, high):
+        @pl.when(first)
+        def _():
+            def send(c, carry):
+                z_copy(c).start()
+                return carry
+
+            lax.fori_loop(low, high, send, 0)
+
+    loads[1].wait()
+    loads[0].wait()
+    send_own(0, FIRST)
 
     entry = start[0] + tm * 2
     line = lax.broadcasted_iota(jnp.int32, (8, 112), 0)
@@ -120,48 +167,10 @@
     GAINS[0] = jnp.broadcast_to(q_gain[...], (128, 64)).T
     GAINS[1] = jnp.broadcast_to(k_gain[...], (128, 64)).T
 
-    pl.semaphore_wait(barrier, len(everyone))
-
-    half = pl.ds(pl.multiple_of(zh * 16, 16), 16)
-    ex_x = copy(traj.at[1 - zh], XR.at[zh], exs.at[0], exr.at[0], other_half)
-    ex_pos = copy(pos, POS.at[y, half], exs.at[1], exr.at[1], other_half)
-    ex_x.start()
-    ex_pos.start()
-    XR[zh] = traj[zh]
-    POS[y, half, :] = pos[...]
-
-    even = x % 2
-    first = jnp.where(core == 0, zl == 3, zl == 0)
-    own = 1 - first.astype(jnp.int32)
-    z_quarter = 2 * core + even
-
-    def rows(quarter, c):
-        return pl.ds(pl.multiple_of(c * CHUNK + quarter * PIECE, 16), PIECE)
-
-    def z_copy(c):
-        at = rows(z_quarter, c)
-        return copy(
-            WB.at[own, at], WB.at[1, at], zs.at[c], zr.at[c], device(z + way, x, core, y)
-        )
-
-    def x_copy(c):
-        at = rows(z_quarter, c)
-        return copy(WB.at[1, at], WB.at[1, at], xs.at[c], xr.at[c], device(z, x + way, core, y))
-
-    def core_copy(c):
-        at = pl.ds(pl.multiple_of(c * CHUNK + core * 2 * PIECE, 16), 2 * PIECE)
-        return copy(WB.at[1, at], WB.at[1, at], cs.at[c], cr.at[c], other_core)
-
-    for load in loads[0:5]:
-        load.wait()
-
-    @pl.when(first)
-    def _():
-        def send(c, carry):
-            z_copy(c).start()
-            return carry
-
-        lax.fori_loop(0, CHUNKS, send, 0)
+    loads[2].wait()
+    loads[3].wait()
+    loads[4].wait()
+    send_own(FIRST, CHUNKS)
 
     def pump_x(c):
         x_copy(c).wait_recv()
@@ -182,11 +191,6 @@
         def _():
             pump_x(c - LAG)
 
-        @pl.when(c == LAG)
-        def _():
-            for one in wo_copies(1):
-                one.start()
-
         return carry
 
     def arrive(c, carry):
@@ -195,29 +199,24 @@
 
     mine = pl.ds(pl.multiple_of(core * 96, 16), 96)
 
+    def wo_copy(part, k):
+        return copy(
+            WB.at[part, pl.ds(pl.multiple_of(WO_AT + core * 96, 16), 96)],
+            WOF.at[y, part, mine],
+            wos.at[part, k],
+            wor.at[part, k],
+            y_peers[k],
+        )
+
+    def wo_forward(part, k):
+        at = WOF.at[(y + 3 - k) % 4, part, mine]
+        return copy(at, at, wfs.at[part, k], wfr.at[part, k], other_core)
+
     def wo_copies(part):
-        return [
-            copy(
-                WB.at[part, pl.ds(pl.multiple_of(WO_AT + core * 96, 16), 96)],
-                WOF.at[y, part, mine],
-                wos.at[part, k],
-                wor.at[part, k],
-                y_peers[k],
-            )
-            for k in range(3)
-        ]
+        return [wo_copy(part, k) for k in range(3)]
 
     def wo_forwards(part):
-        return [
-            copy(
-                WOF.at[(y + 3 - k) % 4, part, mine],
-                WOF.at[(y + 3 - k) % 4, part, mine],
-                wfs.at[part, k],
-                wfr.at[part, k],
-                other_core,
-            )
-            for k in range(3)
-        ]
+        return [wo_forward(part, k) for k in range(3)]
 
     loads[6].wait()
     loads[7].wait()
@@ -261,7 +260,8 @@
             jnp.where(hop == 2, values[1], jnp.where(hop == 3, values[2], values[3])),
         )
 
-    ready, before, middle = by_hop(0, 6, 12, 12), by_hop(15, 14, 9, 7), by_hop(15, 15, 15, 10)
+    ready = by_hop(6, 6, 12, 12)
+    before, between, middle = by_hop(18, 16, 13, 10), by_hop(18, 18, 15, 11), by_hop(21, 21, 21, 16)
     lax.fori_loop(0, ready, only_prompt, 0)
     pump(0, 0)
 
@@ -273,7 +273,7 @@
     def state_copies(r):
         return [
             copy(XIN.at[r, y], XIN.at[r, y], gs.at[r, k], gr.at[r, k], y_peers[k])
-            for k in range(3)
+            for k in FAR_FIRST
         ]
 
     pos_copies = [
@@ -281,20 +281,19 @@
     ]
     for one in state_copies(0) + pos_copies:
         one.start()
+    def pump_prompt(c, carry):
+        pump(c, carry)
+
+        @pl.when(ready + c - 1 < 12)
+        def _():
+            prompt(ready + c - 1)
+
+        return carry
+
+    lax.fori_loop(1, 4, pump_prompt, 0)
     for one in wo_copies(0):
         one.start()
-
-    def pump_prompt(c, carry):
-        pump(c, carry)
-
-        @pl.when(ready + c - 1 < 12)
-        def _():
-            prompt(ready + c - 1)
-
-        return carry
-
-    lax.fori_loop(1, before, pump_prompt, 0)
-    lax.fori_loop(jnp.minimum(ready + before - 1, 12), 12, only_prompt, 0)
+    lax.fori_loop(4, before, pump_prompt, 0)
     loads[8].wait()
     loads[9].wait()
     loads[10].wait()
@@ -302,6 +301,9 @@
         one.wait()
 
     own_rows = pl.ds(pl.multiple_of(y * 32, 32), 32)
+    their_rows = [
+        pl.ds(pl.multiple_of(((y + k + 1) % 4) * 32, 32), 32) for k in range(3)
+    ]
     start_slot = jnp.logical_and(tm == 0, zh == 0)
 
     def mod(k):
@@ -324,7 +326,9 @@
                 CKN[1, i] = CRECV[at, :].astype(F32).T.astype(BF16)
             CVT[0] = CS[zh, 192:384, :]
             CVT[1] = CRECV[192:384, :]
-            lax.fori_loop(1, 4, arrive, 0)
+            lax.fori_loop(0, FIRST, arrive, 0)
+            for k in (0, 2):
+                wo_copy(1, k).start()
 
         parts = []
 
@@ -338,18 +342,27 @@
                     atr.at[r, p, k],
                     y_peers[k],
                 )
-                for k in range(3)
+                for k in FAR_FIRST
             ]
 
         def send_heads(p):
             AB[r, y, :, p * 128 : (p + 1) * 128] = jnp.concatenate(parts, axis=0).T.astype(BF16)
-            for one in head_copies(p):
-                one.start()
             parts.clear()
+
+            @pl.when(r > 0)
+            def _():
+                for one in head_copies(p):
+                    one.start()
 
         attended = [head_copies(p) for p in range(3)]
         for s in range(2):
-            joint = nt(WB[s, HEADS_AT:UP_AT, :], N[...])
+            if s == 1:
+
+                @pl.when(r == 0)
+                def _():
+                    lax.fori_loop(before, between, pump, 0)
+
+            joint = nt(WB[s, HEADS_AT:WO_AT, :], N[...])
             query = head_norm_t(joint[:192], GAINS[0]).astype(BF16)
             keys = head_norm_t(joint[192:384], GAINS[1])
             values = joint[384:].astype(BF16)
@@ -367,19 +380,49 @@
 
         @pl.when(r == 0)
         def _():
-            for one, forward in zip(wo_copies(0), wo_forwards(0)):
+            ACC[...] = nn(AB[r, y, :, 0:192], WB[0, WO_AT:UP_AT, :]) + nn(
+                AB[r, y, :, 192:384], WB[1, WO_AT:UP_AT, :]
+            )
+            RSS[1] = ACC[...].astype(BF16)
+            mixed = [
+                copy(RSS.at[1, their_rows[k]], RSB.at[3, k], mxs.at[0, k], mxr.at[0, k], y_peers[k])
+                for k in FAR_FIRST
+            ]
+            for one in mixed:
+                one.start()
+            lax.fori_loop(between, middle, pump, 0)
+            for one in mixed:
                 one.wait_recv()
-                forward.start()
-            lax.fori_loop(before, middle, pump, 0)
-            lax.fori_loop(0, 1, arrive, 0)
+            total = ACC[own_rows, :]
+            for k in range(3):
+                total = total + RSB[3, k].astype(F32)
+            H[own_rows, :] = H[own_rows, :] + mod(2) * total
+            ln_rows(H, N, mod(3), mod(4), y * 32, 32)
+            normed = [
+                copy(N.at[own_rows], N.at[own_rows], mxs.at[1, k], mxr.at[1, k], y_peers[k])
+                for k in FAR_FIRST
+            ]
+            for one in normed:
+                one.start()
+            lax.fori_loop(middle, STEPS, pump, 0)
+            for part, k in ((0, 0), (0, 2), (0, 1), (1, 0), (1, 2)):
+                wo_copy(part, k).wait_recv()
+                wo_forward(part, k).start()
             fill = pltpu.make_async_copy(
                 WB.at[1, pl.ds(WO_AT, 192)], WOF.at[y, 1], local.at[11]
             )
             fill.start()
-            for one, forward in zip(wo_copies(1), wo_forwards(1)):
+            lax.fori_loop(FIRST, CHUNKS, arrive, 0)
+            fill.wait()
+            for one in normed:
                 one.wait_recv()
-                forward.start()
-            fill.wait()
+            for one in mixed + normed:
+                one.wait_send()
+
+        @pl.when(r == 1)
+        def _():
+            wo_copy(1, 1).wait_recv()
+            wo_forward(1, 1).start()
             for part in range(2):
                 for forward in wo_forwards(part):
                     forward.wait_recv()
@@ -387,18 +430,15 @@
         def project(k):
             return nn(AB[r, (y + k) % 4], WOF[(y + k) % 4].reshape(384, 1536))
 
-        ACC[...] = project(0)
-        for k, i in ((1, 2), (3, 0), (2, 1)):
-            for p in range(3):
-                attended[p][i].wait_recv()
-            ACC[...] += project(k)
-        H[...] = H[...] + mod(2) * ACC[...]
-        ln_rows(H, N, mod(3), mod(4), 0, 128)
-
-        @pl.when(r == 0)
-        def _():
-            lax.fori_loop(middle, STEPS, pump, 0)
-            lax.fori_loop(4, 8, arrive, 0)
+        @pl.when(r > 0)
+        def _():
+            ACC[...] = project(0)
+            for k, i in ((1, 2), (3, 1), (2, 0)):
+                for p in range(3):
+                    attended[p][i].wait_recv()
+                ACC[...] += project(k)
+            H[...] = H[...] + mod(2) * ACC[...]
+            ln_rows(H, N, mod(3), mod(4), 0, 128)
 
         active = []
         for s in range(2):
@@ -406,10 +446,6 @@
                 N[:, 768:1536], WB[s, UP_AT:DOWN_AT, 768:1536]
             )
             active.append(jax.nn.gelu(hidden, approximate=True).astype(BF16))
-
-        @pl.when(r == 0)
-        def _():
-            lax.fori_loop(8, CHUNKS, arrive, 0)
 
         summed = []
         for p in range(2):
@@ -418,13 +454,10 @@
                 active[1], WB[1, DOWN_AT:ALL_ROWS, at]
             )
             ACC[:, at] = total
-            RSS[:, at] = total.astype(BF16)
-            for k in range(3):
+            RSS[0, :, at] = total.astype(BF16)
+            for k in FAR_FIRST:
                 one = copy(
-                    RSS.at[
-                        pl.ds(pl.multiple_of(((y + k + 1) % 4) * 32, 32), 32),
-                        pl.ds(p * 768, 768),
-                    ],
+                    RSS.at[0, their_rows[k], pl.ds(p * 768, 768)],
                     RSB.at[r, k, :, pl.ds(p * 768, 768)],
                     rss.at[r, p, k],
                     rsr.at[r, p, k],
@@ -434,6 +467,11 @@
                 summed.append(one)
         for one in summed:
             one.wait_recv()
+
+        @pl.when(r == 0)
+        def _():
+            wo_copy(1, 1).start()
+
         contract = ACC[own_rows, :]
         for k in range(3):
             contract = contract + RSB[r, k].astype(F32)
@@ -462,7 +500,7 @@
         SUMS[r, 1] = below + both_halves
         XS[r, x, core] = below
         along_x = []
-        for k in range(1, 8):
+        for k in (4, 5, 2, 3, 6, 7, 1):
             to_x, to_core = (x + k // 2) % 4, (core + k) % 2
             later = (2 * to_x + to_core > 2 * x + core).astype(jnp.int32)
             one = copy(
@@ -495,8 +533,14 @@
             for s, total in enumerate([base + lower, base + both_halves]):
                 out[s] = -jnp.where(upper, total[:, 64:128], total[:, 0:64])
 
-        for one in sum(attended, []) + summed + along_x + along_z:
+        for one in summed + along_x + along_z:
             one.wait_send()
+
+        @pl.when(r > 0)
+        def _():
+            for one in sum(attended, []):
+                one.wait_send()
+
         return carry
 
     lax.fori_loop(0, ROUNDS, one_round, 0)
@@ -558,8 +602,8 @@
             pltpu.VMEM((128, 1536), BF16),
             pltpu.VMEM((128, 1536), F32),
             pltpu.VMEM((R, 4, 128, 384), BF16),
-            pltpu.VMEM((128, 1536), BF16),
-            pltpu.VMEM((R, 3, 32, 1536), BF16),
+            pltpu.VMEM((2, 128, 1536), BF16),
+            pltpu.VMEM((R + 1, 3, 32, 1536), BF16),
             pltpu.VMEM((R, 8, 16, 128), F32),
             pltpu.VMEM((R, 2, 16, 128), F32),
             pltpu.VMEM((R, 4, 2, 16, 128), F32),
@@ -594,6 +638,8 @@
             dma((R, 7)),
             dma((R, 7)),
             dma((R, 7)),
+            dma((2, 3)),
+            dma((2, 3)),
         ],
         compiler_params=pltpu.CompilerParams(
             collective_id=0, has_side_effects=True, vmem_limit_bytes=56 << 20

time: 149 us -> 143 us (0.960)
  Pallas kernels: 147 us -> 141 us
    pallas_call x1, Pallas kernels: 147 us -> 141 us  [per_device(): pl.pallas_call(kernel, out_shape=jax.ShapeDtypeStruct((2, 16, 64), F32),...]
where the time goes in v3:
time: 143 us
  Pallas kernels  141 us (99%)
    pallas_call x1, Pallas kernels, per_device(): pl.pallas_call(kernel, out_shape=jax.ShapeDtypeStruct((2, 16, 64), F32),...  141 us

profile of v3, /device:TPU:1, one launch (start us, length us, event | category | flops | bytes accessed | tf_op | source)
XLA Modules:
  0.0 142.9 jit_solution(15530400781874113290)
XLA Ops:
  0.7 140.9 %picard.1 = f32[2,16,64]{2,1,0:T(8,128)} custom-call(f32[2,16,64]{2,1,0:T(8,128)} %traj.1, s32[1]{0:T(128)S(6)} %copy.17.start, f32[1,112]{1,0:T(1,128)} %bitcast.15, bf16[10,112,1536]{2,1,0:T(8,128)(2,1)} %bitcast.11, bf16[128,1536]{1,0:T(8,128)(2,1)} %ctx.1, bf16[16,1536]{1,0:T(8,128)(2,1)} %pos.1, bf16[64,1536]{1,0:T(8,128)(2,1)} %patch.1, ...), custom_call_target="tpu_custom_call" | custom-call | flops 7000000000 | bytes 10000000 | tf_op jit(solution)/shard_map/picard/pallas_call | solution.py:583
  141.6 1.3 copy.18

commit v4 on v3

--- a/solution.py
+++ b/solution.py
@@ -13,7 +13,7 @@
 F32 = jnp.float32
 BF16 = jnp.bfloat16
 
-LAG = 3
+LAG = 4
 CHUNKS = 18
 CHUNK = 128
 STEPS = CHUNKS + LAG
@@ -261,7 +261,7 @@
         )
 
     ready = by_hop(6, 6, 12, 12)
-    before, between, middle = by_hop(18, 16, 13, 10), by_hop(18, 18, 15, 11), by_hop(21, 21, 21, 16)
+    before, between, middle = by_hop(18, 16, 13, 11), by_hop(18, 18, 15, 12), by_hop(22, 22, 22, 17)
     lax.fori_loop(0, ready, only_prompt, 0)
     pump(0, 0)
 

time: 143 us -> 143 us (level)
  no operation moved by 1% of the time
where the time goes in v4:
time: 143 us
  Pallas kernels  141 us (99%)
    pallas_call x1, Pallas kernels, per_device(): pl.pallas_call(kernel, out_shape=jax.ShapeDtypeStruct((2, 16, 64), F32),...  141 us

profile of v4, /device:TPU:1, one launch (start us, length us, event | category | flops | bytes accessed | tf_op | source)
XLA Modules:
  0.0 142.6 jit_solution(1983254027784681556)
XLA Ops:
  0.7 140.6 %picard.1 = f32[2,16,64]{2,1,0:T(8,128)} custom-call(f32[2,16,64]{2,1,0:T(8,128)} %traj.1, s32[1]{0:T(128)S(6)} %copy.17.start, f32[1,112]{1,0:T(1,128)} %bitcast.15, bf16[10,112,1536]{2,1,0:T(8,128)(2,1)} %bitcast.11, bf16[128,1536]{1,0:T(8,128)(2,1)} %ctx.1, bf16[16,1536]{1,0:T(8,128)(2,1)} %pos.1, bf16[64,1536]{1,0:T(8,128)(2,1)} %patch.1, ...), custom_call_target="tpu_custom_call" | custom-call | flops 7000000000 | bytes 10000000 | tf_op jit(solution)/shard_map/picard/pallas_call | solution.py:583
  141.3 1.3 copy.18
